TPU v7x, 32 devices: a whole 2x2x4 slice. The times are simulated.
32 devices in a mesh: rep: 2 (over y), ad: 4 (over z), tp: 4 (over x, core).
Axes of the slice: x: 2, y: 2, z: 4, core: 2. Of those that a mesh axis runs over, the one named last changes fastest.
Arguments:
- tokens: bfloat16 [2048, 8192], P(('rep', 'ad'), 'tp'), parts along dimension 0, may hold values from -6 to 6
- request_adapter: int32 [2048], P(('rep', 'ad')), parts along dimension 0, may hold values from 0 to 31, as said below
- adapter_page_lookup: int32 [64], P('rep'), parts along dimension 0, may hold values from 0 to 31, as said below
- base_key_value_weight: bfloat16 [8192, 2048], P(None, 'tp'), may hold values from -0.0625 to 0.0625
- down_factor_pages: bfloat16 [64, 8192, 64], P(('rep', 'ad'), 'tp'), parts along dimension 0, may hold values from -0.0625 to 0.0625
- up_factor_pages: bfloat16 [64, 64, 2048], P(('rep', 'ad'), None, 'tp'), parts along dimension 0, may hold values from -0.75 to 0.75
Outputs:
- kv_out: bfloat16 [2048, 2048], P(('rep', 'ad'), 'tp'), parts along dimension 0
There are 2 independent parts, one for each index of `rep`. A program takes and returns all parts, laid end to end along the dimension named above; an argument that names none is the same for every part. Nothing has to cross between parts.
Inputs may be any that keep to these rules, and one draw needn't show every extreme that they name: `request_adapter`: within each aligned block of 256 requests, at most 128 requests name adapters whose pages lie in one aligned block of 8 pages; one block of pages receives exactly 128 requests from every block of requests. `adapter_page_lookup`: A permutation.
All inputs are finite; a program needn't handle non-finite values.
Results may differ from a plain program's by a relative error of at most 0.0049.
Values may be sent and summed in bfloat16 or wider, within the bound.
A program may use at most 64 MiB of HBM per device.

v0:
```python
import jax
import jax.numpy as jnp
from jax import lax
from jax.sharding import PartitionSpec as P


def apply_adapter(input_rows, which_adapter, down_factor_pages, up_factor_pages):
    page_holders, entries_list, width = input_rows.shape
    page_entries = down_factor_pages.shape[0]
    flattened_rows = input_rows.reshape(page_holders * entries_list, width)
    select = (
        which_adapter.reshape(-1)[:, None] == jnp.arange(page_entries, dtype=jnp.int32)[None, :]
    ).astype(jnp.float32)
    first_factor = jnp.einsum(
        "gh,ehb->geb", flattened_rows, down_factor_pages, preferred_element_type=jnp.float32
    )
    partial_rank = jnp.einsum("sar,sa->sr", first_factor, select)
    shrink = lax.psum(partial_rank, "tp").astype(jnp.bfloat16)
    spread_rows = select.astype(jnp.bfloat16)[:, :, None] * shrink[:, None, :]
    adapter_update = jnp.einsum(
        "jbk,bkh->jh", spread_rows, up_factor_pages, preferred_element_type=jnp.float32
    )
    return adapter_update.astype(jnp.bfloat16).reshape(
        page_holders, entries_list, up_factor_pages.shape[2]
    )


def shards(
    tokens,
    request_adapter,
    adapter_page_lookup,
    base_key_value_weight,
    down_factor_pages,
    up_factor_pages,
):
    page_holders = lax.axis_size("ad")
    token_rows, width = tokens.shape
    page_entries = down_factor_pages.shape[0]
    columns = base_key_value_weight.shape[1]
    capacity = max(2, min(4 * token_rows // page_holders, token_rows // 2))
    base = jnp.dot(
        lax.all_gather(tokens, "tp", axis=1, tiled=True),
        base_key_value_weight,
        preferred_element_type=jnp.float32,
    )
    catalog = jnp.arange(adapter_page_lookup.shape[0], dtype=jnp.int32)
    matches = request_adapter[:, None] == catalog[None, :]
    page = jnp.sum(jnp.where(matches, adapter_page_lookup[None, :], 0), axis=1)
    target = page // page_entries
    within = page % page_entries
    onehot = (target[:, None] == jnp.arange(page_holders, dtype=jnp.int32)[None, :]).astype(
        jnp.int32
    )
    before = jnp.cumsum(onehot, axis=0) - onehot
    position = jnp.sum(before * onehot, axis=1)
    place = target * capacity + position
    send_rows = jnp.zeros((page_holders * capacity, width), jnp.bfloat16).at[place].set(tokens)
    send_rows = send_rows.reshape(page_holders, capacity, width)
    send_which = jnp.full((page_holders * capacity,), -1, jnp.int32).at[place].set(within)
    send_which = send_which.reshape(page_holders, capacity)
    received_token_rows, received_adapter = (
        lax.all_to_all(send_rows, "ad", split_axis=0, concat_axis=0, tiled=True),
        lax.all_to_all(send_which, "ad", split_axis=0, concat_axis=0, tiled=True),
    )
    returned_rows = apply_adapter(
        received_token_rows, received_adapter, down_factor_pages, up_factor_pages
    )
    returned = lax.all_to_all(returned_rows, "ad", split_axis=0, concat_axis=0, tiled=True)
    adapter_update = returned.reshape(page_holders * capacity, columns)[place]
    return (base + adapter_update.astype(jnp.float32)).astype(jnp.bfloat16)


def solution(mesh):
    return jax.shard_map(
        shards,
        mesh=mesh,
        in_specs=(
            P(("rep", "ad"), "tp"),
            P(("rep", "ad")),
            P("rep"),
            P(None, "tp"),
            P(("rep", "ad"), "tp", None),
            P(("rep", "ad"), None, "tp"),
        ),
        out_specs=P(("rep", "ad"), "tp"),
        check_vma=False,
    )
```

profile of v0, /device:TPU:0, one launch (start us, length us, event | category | flops | bytes accessed | tf_op | source)
XLA Modules:
  0.0 125.7 jit_solution(12384776847864058803)
XLA Ops:
  6.5 0.0 copy-start
  6.5 0.0 all-gather.2.cloned.1.call-start
  6.5 0.7 all-gather.2.cloned.1.call-update
  7.3 0.8 select_reduce_fusion
  8.1 1.2 reduce-window.6
  9.3 0.1 slice.10
  9.4 0.1 copy.11
  9.5 0.1 copy.12
  9.6 0.1 add_bitcast_fusion
  9.7 2.0 %scatter_custom_fusion = s32[512]{0:T(512)} fusion(s32[256]{0:T(256)S(1)} %bitcast.55, s32[256]{0:T(256)S(1)} %get-tuple-element.7, s32[]{:T(128)} %constant.32.clone.1), kind=kCustom, calls=%fused_computation.41 | custom fusion | bytes 2052 | tf_op jit(solution)/shard_map/scatter | solution.py:59
  11.7 6.3 %all-to-all-start = ((s32[4,1,128]{2,1,0:T(1,128)}), s32[4,1,128]{2,1,0:T(1,128)S(1)}, u32[]{:S(2)}, u32[]{:S(2)}) async-start(s32[4,1,128]{2,1,0:T(1,128)} %bitcast.6), calls=%async_computation | async-start | bytes 4096 | tf_op jit(solution)/shard_map/all_to_all | solution.py:63
  18.0 4.5 %scatter_custom_fusion.1 = bf16[512,2048]{1,0:T(8,128)(2,1)} fusion(s32[256]{0:T(256)S(1)} %bitcast.56, bf16[256,2048]{1,0:T(8,128)(2,1)} %param.6, bf16[]{:T(256)} %constant.40.clone.1), kind=kCustom, calls=%fused_computation.8 | custom fusion | bytes 2097664 | tf_op jit(solution)/shard_map/scatter | solution.py:57
  22.6 0.9 all-to-all-done
  23.5 4.5 %all-to-all-start.1 = ((bf16[4,128,2048]{2,1,0:T(8,128)(2,1)}), bf16[4,128,2048]{2,1,0:T(8,128)(2,1)}, u32[]{:S(2)}, u32[]{:S(2)}) async-start(bf16[4,128,2048]{2,1,0:T(8,128)(2,1)} %bitcast.51), calls=%async_computation.1 | async-start | bytes 4194304 | tf_op jit(solution)/shard_map/all_to_all | solution.py:62
  28.0 47.4 %all-to-all-done.1 = bf16[4,128,2048]{2,1,0:T(8,128)(2,1)} async-done(((bf16[4,128,2048]{2,1,0:T(8,128)(2,1)}), bf16[4,128,2048]{2,1,0:T(8,128)(2,1)}, u32[]{:S(2)}, u32[]{:S(2)}) %all-to-all-start.1) | async-done | bytes 2097184 | tf_op jit(solution)/shard_map/all_to_all | solution.py:62
  75.4 0.0 copy-done
  75.4 0.0 copy-start.1
  75.4 2.9 %fusion.14 = f32[512,512]{0,1:S(1)} fusion(bf16[512,2048]{1,0:T(8,128)(2,1)} %bitcast.9, bf16[2048,512]{0,1:T(8,128)(2,1)S(1)} %bitcast.49), kind=kOutput, calls=%fused_computation.45 | convolution fusion | flops 1073741824 | bytes 5242880
  78.3 0.1 multiply_reduce_fusion
  78.4 11.6 %all-reduce.1 = bf16[512,64]{0,1:T(8,128)(2,1)S(1)} all-reduce(f32[512,64]{0,1:T(8,128)S(1)} %multiply_reduce_fusion), channel_id=1, replica_groups=mesh['rep'=2,'ad'=4,'tp'=4] {'tp'}, use_global_device_ids=true, to_apply=%region_6.7 | all-reduce | flops 32768 | bytes 196608 | tf_op jit(solution)/shard_map/psum | solution.py:18
  90.1 0.0 copy-done.1
  90.1 1.3 %fusion = bf16[512,512]{1,0:T(8,128)(2,1)} fusion(bf16[8,64,512]{2,1,0:T(8,128)(2,1)S(1)} %copy-done.1, bf16[512,64]{0,1:T(8,128)(2,1)S(1)} %all-reduce.1, bf16[512,8]{0,1:T(8,128)(2,1)S(1)} %get-tuple-element.5), kind=kOutput, calls=%fused_computation.4 | convolution fusion | flops 268959744 | bytes 1122304 | tf_op jit(solution)/shard_map/jbk,bkh->jh/dot_general | solution.py:20
  91.3 3.5 %all-to-all-start.2 = ((bf16[4,128,512]{2,1,0:T(8,128)(2,1)}), bf16[4,128,512]{2,1,0:T(8,128)(2,1)S(1)}, u32[]{:S(2)}, u32[]{:S(2)}) async-start(bf16[4,128,512]{2,1,0:T(8,128)(2,1)} %bitcast.14), calls=%async_computation.2 | async-start | bytes 1048576 | tf_op jit(solution)/shard_map/all_to_all | solution.py:68
  94.8 15.1 %all-to-all-done.2 = bf16[4,128,512]{2,1,0:T(8,128)(2,1)S(1)} async-done(((bf16[4,128,512]{2,1,0:T(8,128)(2,1)}), bf16[4,128,512]{2,1,0:T(8,128)(2,1)S(1)}, u32[]{:S(2)}, u32[]{:S(2)}) %all-to-all-start.2) | async-done | bytes 524320 | tf_op jit(solution)/shard_map/all_to_all | solution.py:68
  109.9 1.2 gather_fusion
  111.1 0.0 all-gather.2.cloned.1.call-done
  111.1 7.7 %fusion.1 = bf16[256,512]{1,0:T(8,128)(2,1)} fusion(bf16[256,8192]{1,0:T(8,128)(2,1)} %all-gather.2.cloned.1.call-done, bf16[8192,512]{1,0:T(8,128)(2,1)} %param.9, bf16[256,512]{1,0:T(8,128)(2,1)S(1)} %gather_fusion), kind=kOutput, calls=%fused_computation.6 | convolution fusion | flops 2147876864 | bytes 13107200 | tf_op jit(solution)/shard_map/dot_general | solution.py:41
  (9 shorter events, 0.1 us)
Async XLA Ops:
  6.5 68.8 %copy-start = (bf16[8,2048,64]{1,2,0:T(8,128)(2,1)S(1)}, bf16[8,2048,64]{1,2,0:T(8,128)(2,1)}, u32[]{:S(2)}) copy-start(bf16[8,2048,64]{1,2,0:T(8,128)(2,1)} %param.10) | copy-start | bytes 6291460
  6.5 104.6 %all-gather.2.cloned.1.call-start = ((), (), s32[]{:S(2)}) async-start(), calls=%async_computation.3 | async-start | bytes 5242880 | tf_op jit(solution)/shard_map/all_gather | solution.py:42
  11.7 11.8 %all-to-all-start = ((s32[4,1,128]{2,1,0:T(1,128)}), s32[4,1,128]{2,1,0:T(1,128)S(1)}, u32[]{:S(2)}, u32[]{:S(2)}) async-start(s32[4,1,128]{2,1,0:T(1,128)} %bitcast.6), calls=%async_computation | async-start | bytes 4096 | tf_op jit(solution)/shard_map/all_to_all | solution.py:63
  23.5 51.9 %all-to-all-start.1 = ((bf16[4,128,2048]{2,1,0:T(8,128)(2,1)}), bf16[4,128,2048]{2,1,0:T(8,128)(2,1)}, u32[]{:S(2)}, u32[]{:S(2)}) async-start(bf16[4,128,2048]{2,1,0:T(8,128)(2,1)} %bitcast.51), calls=%async_computation.1 | async-start | bytes 4194304 | tf_op jit(solution)/shard_map/all_to_all | solution.py:62
  75.4 14.7 %copy-start.1 = (bf16[8,64,512]{2,1,0:T(8,128)(2,1)S(1)}, bf16[8,64,512]{2,1,0:T(8,128)(2,1)}, u32[]{:S(2)}) copy-start(bf16[8,64,512]{2,1,0:T(8,128)(2,1)} %param.11) | copy-start | bytes 1572868
  91.3 18.6 %all-to-all-start.2 = ((bf16[4,128,512]{2,1,0:T(8,128)(2,1)}), bf16[4,128,512]{2,1,0:T(8,128)(2,1)S(1)}, u32[]{:S(2)}, u32[]{:S(2)}) async-start(bf16[4,128,512]{2,1,0:T(8,128)(2,1)} %bitcast.14), calls=%async_computation.2 | async-start | bytes 1048576 | tf_op jit(solution)/shard_map/all_to_all | solution.py:68
Sparse Core Ops, SparseCore 0:
  8.9 37.2 all-gather.1
where the time goes:
time: 126 us
  waiting for transfers between devices  64.2 us (51%)
  starting transfers between devices  14.2 us (11%)
  between operations  13.5 us (11%)
  matrix products  11.9 us (9%)
  blocking collectives  11.6 us (9%)
  local copies, waits for them, and re-layouts  7.94 us (6%)
  other arithmetic  2.32 us (2%)
    all_to_all x1, waiting for transfers between devices, shards(): lax.all_to_all(send_rows, 'ad', split_axis=0, concat_axis=0, tiled=True)  47.4 us
    all_to_all x1, waiting for transfers between devices, shards(): lax.all_to_all(returned_rows, 'ad', split_axis=0, concat_axis=0, tiled=True)  15.1 us
    psum x1, blocking collectives, apply_adapter(): shrink = lax.psum(partial_rank, 'tp').astype(jnp.bfloat16)  11.6 us
    dot_general x1, matrix products, shards(): jnp.dot(lax.all_gather(tokens, 'tp', axis=1, tiled=True), base_key_value_...  7.69 us
    all_to_all x1, starting transfers between devices, shards(): lax.all_to_all(send_which, 'ad', split_axis=0, concat_axis=0, tiled=True)  6.32 us
    scatter x1, local copies, waits for them, and re-layouts, shards(): jnp.zeros((page_holders * capacity, width), jnp.bfloat16).at[place]  4.55 us
    all_to_all x1, starting transfers between devices, shards(): lax.all_to_all(send_rows, 'ad', split_axis=0, concat_axis=0, tiled=True)  4.45 us
    all_to_all x1, starting transfers between devices, shards(): lax.all_to_all(returned_rows, 'ad', split_axis=0, concat_axis=0, tiled=True)  3.47 us
  transfers between devices with their start and end apart: 4, of which 3 were waited for; matrix products, arithmetic and copies ran while one was open for 11% of the time, Pallas kernels for 0%

commit v1 on v0

v1 whole, which is shorter than its diff:
```python
import functools

import jax
import jax.numpy as jnp
from jax import lax
from jax.experimental import pallas as pl
from jax.experimental.pallas import tpu as pltpu
from jax.sharding import PartitionSpec as P

MESH = pl.DeviceIdType.MESH
LANES = 128
DEPTH = 512


def kernel(
    n, rank, send_ref, which_ref, tok_ref, comb_ref, up_ref, w_hbm, down_hbm, out_ref,
    recv, rwhich, gath, w, down, dcat, acc, part, dsend, ret,
    local_sem, row_send, row_recv, which_send, which_recv,
    tok_send, tok_recv, part_send, part_recv, ret_send, ret_recv,
):
    me, t = lax.axis_index("ad"), lax.axis_index("tp")
    sibling = t + 1 - 2 * lax.rem(t, 2)
    across = lax.rem(t + 2, 4)
    diagonal = lax.rem(sibling + 2, 4)
    cap, wide = send_ref.shape[1], dcat.shape[1]
    width = tok_ref.shape[1]

    barrier = pltpu.get_barrier_semaphore()

    @pl.loop(1, n)
    def _(s):
        pl.semaphore_signal(barrier, inc=1, device_id={"ad": lax.rem(me + s, n)}, device_id_type=MESH)

    for s in range(1, 4):
        pl.semaphore_signal(barrier, inc=1, device_id={"tp": lax.rem(t + s, 4)}, device_id_type=MESH)
    down_copy = pltpu.make_async_copy(down_hbm, down, local_sem.at[0])
    w_copy = pltpu.make_async_copy(w_hbm, w, local_sem.at[1])
    down_copy.start()
    w_copy.start()
    pl.semaphore_wait(barrier, n - 1 + 3)

    def rows_to(j):
        return pltpu.make_async_remote_copy(
            src_ref=send_ref.at[j], dst_ref=recv.at[me], send_sem=row_send.at[j],
            recv_sem=row_recv.at[me], device_id={"ad": j}, device_id_type=MESH)

    def rows_from(j):
        return pltpu.make_async_remote_copy(
            src_ref=send_ref.at[j], dst_ref=recv.at[j], send_sem=row_send.at[j],
            recv_sem=row_recv.at[j], device_id={"ad": j}, device_id_type=MESH)

    def which_copy(j, slot):
        return pltpu.make_async_remote_copy(
            src_ref=which_ref.at[j], dst_ref=rwhich.at[slot], send_sem=which_send.at[j],
            recv_sem=which_recv.at[slot], device_id={"ad": j}, device_id_type=MESH)

    def token_copy(k, src, slot, to):
        return pltpu.make_async_remote_copy(
            src_ref=src, dst_ref=gath.at[slot], send_sem=tok_send.at[k],
            recv_sem=tok_recv.at[k], device_id={"tp": to}, device_id_type=MESH)

    def part_copy(k, j, slot):
        return pltpu.make_async_remote_copy(
            src_ref=part.at[t, j], dst_ref=part.at[slot, j], send_sem=part_send.at[k, j],
            recv_sem=part_recv.at[slot, j], device_id={"tp": lax.rem(t + k, 4)}, device_id_type=MESH)

    def part_from(k, j):
        slot = lax.rem(t + 4 - k, 4)
        return pltpu.make_async_remote_copy(
            src_ref=part.at[t, j], dst_ref=part.at[slot, j], send_sem=part_send.at[k, j],
            recv_sem=part_recv.at[slot, j], device_id={"tp": slot}, device_id_type=MESH)

    def ret_copy(j, slot):
        return pltpu.make_async_remote_copy(
            src_ref=dsend.at[j], dst_ref=ret.at[slot], send_sem=ret_send.at[j],
            recv_sem=ret_recv.at[slot], device_id={"ad": j}, device_id_type=MESH)

    @pl.loop(1, n)
    def _(s):
        j = lax.rem(me + s, n)
        which_copy(j, me).start()
        rows_to(j).start()

    token_copy(1, tok_ref, t, across).start()
    token_copy(0, tok_ref, t, sibling).start()

    down_copy.wait()
    for e in range(down.shape[0]):
        dcat[:, e * rank : (e + 1) * rank] = down[e]

    lane_page = (lax.broadcasted_iota(jnp.int32, (cap, wide), 1) // rank).astype(jnp.float32)
    same = lax.broadcasted_iota(jnp.int32, (cap, cap), 0) == lax.broadcasted_iota(jnp.int32, (cap, cap), 1)

    def page_mask(tile):
        line = jnp.broadcast_to(tile[0:1, :].astype(jnp.float32), (cap, cap))
        spread = jnp.where(same, line, 0.0).astype(jnp.bfloat16)
        column = jnp.dot(spread, jnp.ones((cap, wide), jnp.bfloat16), preferred_element_type=jnp.float32)
        return column == lane_page

    def partial(rows, tile, j):
        first = jnp.dot(rows, dcat[...], preferred_element_type=jnp.float32)
        first = jnp.where(page_mask(tile), first, 0.0)
        total = first[:, :LANES]
        for k in range(1, wide // LANES):
            total = total + first[:, k * LANES : (k + 1) * LANES]
        part[t, j] = total
        for k in range(1, 4):
            part_copy(k, j, t).start()

    def update(tile, j):
        for k in range(1, 4):
            part_from(k, j).wait_recv()
        shrink = part[0, j] + part[1, j] + part[2, j] + part[3, j]
        spread = jnp.concatenate([shrink] * (wide // LANES), axis=1)
        spread = jnp.where(page_mask(tile), spread, 0.0).astype(jnp.bfloat16)
        return jnp.dot(spread, up_ref[...], preferred_element_type=jnp.float32).astype(jnp.bfloat16)

    partial(send_ref[me], which_ref[me], me)

    acc[...] = jnp.zeros_like(acc)
    w_copy.wait()

    def add_base(block, owner):
        @pl.loop(0, width // DEPTH)
        def _(i):
            at = pl.multiple_of(i * DEPTH, DEPTH)
            row = pl.multiple_of(owner * width + i * DEPTH, DEPTH)
            acc[...] += jnp.dot(
                block[:, pl.ds(at, DEPTH)], w[pl.ds(row, DEPTH), :], preferred_element_type=jnp.float32)

    add_base(tok_ref, t)
    token_copy(0, tok_ref, sibling, sibling).wait_recv()
    add_base(gath.at[sibling], sibling)
    token_copy(1, tok_ref, across, across).wait_recv()
    token_copy(2, gath.at[across], across, sibling).start()
    add_base(gath.at[across], across)
    token_copy(2, gath.at[across], diagonal, sibling).wait_recv()
    add_base(gath.at[diagonal], diagonal)
    ret[me] = update(which_ref[me], me)

    @pl.loop(1, n)
    def _(s):
        j = lax.rem(me + s, n)
        which_copy(j, j).wait_recv()
        rows_from(j).wait_recv()
        partial(recv[j], rwhich[j], j)

    @pl.loop(1, n)
    def _(s):
        j = lax.rem(me + s, n)
        dsend[j] = update(rwhich[j], j)
        ret_copy(j, me).start()

    @pl.loop(1, n)
    def _(s):
        j = lax.rem(me + s, n)
        ret_copy(j, j).wait_recv()

    back = ret[...].reshape(n * cap, out_ref.shape[1])
    change = jnp.dot(comb_ref[...], back, preferred_element_type=jnp.float32)
    out_ref[...] = (acc[...] + change).astype(out_ref.dtype)

    @pl.loop(1, n)
    def _(s):
        j = lax.rem(me + s, n)
        which_copy(j, me).wait_send()
        rows_to(j).wait_send()
        ret_copy(j, me).wait_send()

    @pl.loop(0, n)
    def _(j):
        for k in range(1, 4):
            part_copy(k, j, t).wait_send()

    token_copy(0, tok_ref, t, sibling).wait_send()
    token_copy(1, tok_ref, t, across).wait_send()
    token_copy(2, gath.at[across], across, sibling).wait_send()


def shards(
    tokens,
    request_adapter,
    adapter_page_lookup,
    base_key_value_weight,
    down_factor_pages,
    up_factor_pages,
):
    n = lax.axis_size("ad")
    token_rows, width = tokens.shape
    pages, _, rank = down_factor_pages.shape
    columns = base_key_value_weight.shape[1]
    wide = pages * rank
    cap = max(16, min(4 * token_rows // n, token_rows // 2))
    slots = n * cap

    catalog = jnp.arange(adapter_page_lookup.shape[0], dtype=jnp.int32)
    matches = request_adapter[:, None] == catalog[None, :]
    page = jnp.sum(jnp.where(matches, adapter_page_lookup[None, :], 0), axis=1)
    target = page // pages
    within = page % pages
    order = jnp.arange(token_rows, dtype=jnp.int32)
    earlier = (target[:, None] == target[None, :]) & (order[None, :] < order[:, None])
    position = jnp.sum(earlier.astype(jnp.int32), axis=1)
    place = target * cap + position
    slot = jnp.arange(slots, dtype=jnp.int32)
    dispatch = slot[:, None] == place[None, :]
    combine = (place[:, None] == slot[None, :]).astype(jnp.bfloat16)
    send = jnp.dot(
        dispatch.astype(jnp.bfloat16), tokens, preferred_element_type=jnp.float32
    ).astype(jnp.bfloat16).reshape(n, cap, width)
    which = jnp.sum(jnp.where(dispatch, within[None, :], 0), axis=1).astype(jnp.bfloat16)
    which = jnp.broadcast_to(which.reshape(n, 1, cap), (n, 16, cap))

    vmem = pl.BlockSpec(memory_space=pltpu.VMEM)
    hbm = pl.BlockSpec(memory_space=pl.ANY)
    bf16, f32 = jnp.bfloat16, jnp.float32
    dma = pltpu.SemaphoreType.DMA
    return pl.pallas_call(
        functools.partial(kernel, n, rank),
        out_shape=jax.ShapeDtypeStruct((token_rows, columns), bf16),
        in_specs=[vmem] * 5 + [hbm] * 2,
        out_specs=vmem,
        scratch_shapes=[
            pltpu.VMEM((n, cap, width), bf16),
            pltpu.VMEM((n, 16, cap), bf16),
            pltpu.VMEM((4, token_rows, width), bf16),
            pltpu.VMEM(base_key_value_weight.shape, bf16),
            pltpu.VMEM(down_factor_pages.shape, bf16),
            pltpu.VMEM((width, wide), bf16),
            pltpu.VMEM((token_rows, columns), f32),
            pltpu.VMEM((4, n, cap, LANES), f32),
            pltpu.VMEM((n, cap, columns), bf16),
            pltpu.VMEM((n, cap, columns), bf16),
            dma((2,)), dma((n,)), dma((n,)), dma((n,)), dma((n,)),
            dma((3,)), dma((3,)), dma((4, n)), dma((4, n)), dma((n,)), dma((n,)),
        ],
        compiler_params=pltpu.CompilerParams(
            collective_id=0, has_side_effects=True, vmem_limit_bytes=52 * 1024 * 1024
        ),
    )(send, which, tokens, combine, up_factor_pages.reshape(wide, columns),
      base_key_value_weight, down_factor_pages)


def solution(mesh):
    return jax.shard_map(
        shards,
        mesh=mesh,
        in_specs=(
            P(("rep", "ad"), "tp"),
            P(("rep", "ad")),
            P("rep"),
            P(None, "tp"),
            P(("rep", "ad"), "tp", None),
            P(("rep", "ad"), None, "tp"),
        ),
        out_specs=P(("rep", "ad"), "tp"),
        check_vma=False,
    )
```

time: 126 us -> 79.9 us (0.63)
  the two profiles are of different devices: /device:TPU:0 before, /device:TPU:17 now
where the time goes in v1:
time: 79.9 us; the launch traced here: 79.7 us
  Pallas kernels  71.1 us (89%)
  local copies, waits for them, and re-layouts  3.9 us (5%)
  matrix products  3.34 us (4%)
  other arithmetic  1.4 us (2%)
    pallas_call x1, Pallas kernels, shards(): pl.pallas_call(functools.partial(kernel, n, rank), out_shape=jax.ShapeDty...  71.1 us
    unnamed x6, local copies, waits for them, and re-layouts  3.89 us
    dot_general x1, matrix products, shards(): jnp.dot(dispatch.astype(jnp.bfloat16), tokens, preferred_element_type=jnp...  3.34 us

profile of v1, /device:TPU:17, one launch (start us, length us, event | category | flops | bytes accessed | tf_op | source)
XLA Modules:
  0.0 79.7 jit_solution(12403472397218735618)
XLA Ops:
  0.0 0.0 copy-start.1
  0.0 0.9 %select_reduce_fusion.1 = s32[256]{0:T(256)S(1)} fusion(s32[32]{0:T(128)} %param.8, s32[256]{0:T(256)} %param.7), kind=kLoop, calls=%fused_computation.9 | loop fusion | flops 24320 | bytes 2176 | tf_op jit(solution)/shard_map/reduce_sum | solution.py:198
  0.9 0.2 convert_reduce_fusion
  1.1 0.2 select_reduce_fusion
  1.3 0.1 fusion.comb_ref
  1.4 0.0 copy-start
  1.4 3.3 %convolution_convert_fusion = bf16[512,2048]{1,0:T(8,128)(2,1)} fusion(bf16[256,2048]{1,0:T(8,128)(2,1)} %tok_ref.1, s32[256]{0:T(256)S(1)} %multiply_add_fusion), kind=kOutput, calls=%fused_computation | convolution fusion | flops 538050560 | bytes 3146752 | tf_op jit(solution)/shard_map/dot_general | solution.py:208
  4.8 0.0 copy-done.1
  4.8 3.2 %copy.8.down_hbm = bf16[8,2048,64]{2,1,0:T(8,128)(2,1)} copy(bf16[8,2048,64]{1,2,0:T(8,128)(2,1)S(1)} %copy-done.1) | data formatting | bytes 4194304 | tf_op args[4]
  8.0 0.0 copy-done
  8.0 71.1 %shard_map.64 = bf16[256,512]{1,0:T(8,128)(2,1)S(1)} custom-call(bf16[4,128,2048]{2,1,0:T(8,128)(2,1)} %bitcast.6, bf16[4,16,128]{2,1,0:T(8,128)(2,1)S(1)} %broadcast_in_dim.30.which_ref, bf16[256,2048]{1,0:T(8,128)(2,1)} %tok_ref.1, bf16[256,512]{1,0:T(8,128)(2,1)S(1)} %fusion.comb_ref, bf16[512,512]{1,0:T(8,128)(2,1)S(1)} %bitcast.5, ...), custom_call_target="tpu_custom_call" | custom-call | tf_op jit(solution)/shard_map/pallas_call | solution.py:218
  79.0 0.7 copy.10
  (4 shorter events, 0.0 us)
Async XLA Ops:
  0.0 4.8 %copy-start.1 = (bf16[8,2048,64]{1,2,0:T(8,128)(2,1)S(1)}, bf16[8,2048,64]{1,2,0:T(8,128)(2,1)}, u32[]{:S(2)}) copy-start(bf16[8,2048,64]{1,2,0:T(8,128)(2,1)} %param.10) | copy-start | bytes 6291460
  1.4 6.5 %copy-start = (bf16[8,64,512]{2,1,0:T(8,128)(2,1)S(1)}, bf16[8,64,512]{2,1,0:T(8,128)(2,1)}, u32[]{:S(2)}) copy-start(bf16[8,64,512]{2,1,0:T(8,128)(2,1)} %param.11) | copy-start | bytes 1572868

commit v2 on v1

v2 whole, which is shorter than its diff:
```python
import functools

import jax
import jax.numpy as jnp
from jax import lax
from jax.experimental import pallas as pl
from jax.experimental.pallas import tpu as pltpu
from jax.sharding import PartitionSpec as P

MESH = pl.DeviceIdType.MESH
LANES = 128
DEPTH = 512
PIECES = 4


def kernel(
    n, pieces, rank, disp_ref, which_ref, tok_ref, comb_ref, up_ref, w_hbm, down_hbm, out_ref,
    send, recv, rwhich, gath, w, down, acc, part, dsend, ret,
    local_sem, row_send, row_recv, which_send, which_recv,
    tok_send, tok_recv, part_send, part_recv, ret_send, ret_recv,
):
    me, t = lax.axis_index("ad"), lax.axis_index("tp")
    sibling = t + 1 - 2 * lax.rem(t, 2)
    across = lax.rem(t + 2, 4)
    diagonal = lax.rem(sibling + 2, 4)
    width, wide, cap = tok_ref.shape[1], down.shape[0], which_ref.shape[2]
    h = cap // pieces
    rows = n * h

    barrier = pltpu.get_barrier_semaphore()

    @pl.loop(1, n)
    def _(s):
        pl.semaphore_signal(barrier, inc=1, device_id={"ad": lax.rem(me + s, n)}, device_id_type=MESH)

    for s in range(1, 4):
        pl.semaphore_signal(barrier, inc=1, device_id={"tp": lax.rem(t + s, 4)}, device_id_type=MESH)
    down_copy = pltpu.make_async_copy(down_hbm, down, local_sem.at[0])
    w_copy = pltpu.make_async_copy(w_hbm, w, local_sem.at[1])
    down_copy.start()
    w_copy.start()

    def pack(c):
        send[c] = jnp.dot(
            disp_ref[c], tok_ref[...], preferred_element_type=jnp.float32
        ).astype(jnp.bfloat16).reshape(n, h, width)
        recv[c, me] = send[c, me]

    pack(0)
    rwhich[me] = which_ref[me]
    pl.semaphore_wait(barrier, n - 1 + 3)

    def rows_copy(c, j, slot):
        return pltpu.make_async_remote_copy(
            src_ref=send.at[c, j], dst_ref=recv.at[c, slot], send_sem=row_send.at[c, j],
            recv_sem=row_recv.at[c, slot], device_id={"ad": j}, device_id_type=MESH)

    def which_copy(j, slot):
        return pltpu.make_async_remote_copy(
            src_ref=which_ref.at[j], dst_ref=rwhich.at[slot], send_sem=which_send.at[j],
            recv_sem=which_recv.at[slot], device_id={"ad": j}, device_id_type=MESH)

    def token_copy(k, src, slot, to):
        return pltpu.make_async_remote_copy(
            src_ref=src, dst_ref=gath.at[slot], send_sem=tok_send.at[k],
            recv_sem=tok_recv.at[k], device_id={"tp": to}, device_id_type=MESH)

    def part_copy(c, k, slot, to):
        return pltpu.make_async_remote_copy(
            src_ref=part.at[t, c], dst_ref=part.at[slot, c], send_sem=part_send.at[k, c],
            recv_sem=part_recv.at[slot, c], device_id={"tp": to}, device_id_type=MESH)

    def ret_copy(c, j, slot):
        return pltpu.make_async_remote_copy(
            src_ref=dsend.at[c, j], dst_ref=ret.at[c, slot], send_sem=ret_send.at[c, j],
            recv_sem=ret_recv.at[c, slot], device_id={"ad": j}, device_id_type=MESH)

    def dispatch(c):
        @pl.loop(1, n)
        def _(s):
            j = lax.rem(me + s, n)
            if c == 0:
                which_copy(j, me).start()
            rows_copy(c, j, me).start()

    dispatch(0)
    token_copy(1, tok_ref, t, across).start()
    token_copy(0, tok_ref, t, sibling).start()
    for c in range(1, pieces):
        pack(c)
        dispatch(c)

    lane_page = (lax.broadcasted_iota(jnp.int32, (rows, wide), 1) // rank).astype(jnp.float32)
    own_lane = lax.broadcasted_iota(jnp.int32, (rows, cap), 1) - lax.rem(
        lax.broadcasted_iota(jnp.int32, (rows, cap), 0), h)

    def page_mask(c):
        lines = jnp.concatenate(
            [jnp.broadcast_to(rwhich[j][0:1, :].astype(jnp.float32), (h, cap)) for j in range(n)], axis=0)
        spread = jnp.where(own_lane == c * h, lines, 0.0).astype(jnp.bfloat16)
        column = jnp.dot(spread, jnp.ones((cap, wide), jnp.bfloat16), preferred_element_type=jnp.float32)
        return column == lane_page

    def partial(c):
        @pl.loop(1, n)
        def _(s):
            j = lax.rem(me + s, n)
            if c == 0:
                which_copy(j, j).wait_recv()
            rows_copy(c, j, j).wait_recv()

        first = lax.dot_general(
            recv[c].reshape(rows, width), down[...], (((1,), (1,)), ((), ())),
            preferred_element_type=jnp.float32)
        first = jnp.where(page_mask(c), first, 0.0)
        total = first[:, :LANES]
        for k in range(1, wide // LANES):
            total = total + first[:, k * LANES : (k + 1) * LANES]
        part[t, c] = total
        for k in range(1, 4):
            part_copy(c, k, t, lax.rem(t + k, 4)).start()

    def update(c):
        for k in range(1, 4):
            slot = lax.rem(t + 4 - k, 4)
            part_copy(c, k, slot, slot).wait_recv()
        shrink = part[0, c] + part[1, c] + part[2, c] + part[3, c]
        spread = jnp.concatenate([shrink] * (wide // LANES), axis=1)
        spread = jnp.where(page_mask(c), spread, 0.0).astype(jnp.bfloat16)
        delta = jnp.dot(spread, up_ref[...], preferred_element_type=jnp.float32).astype(jnp.bfloat16)
        dsend[c] = delta.reshape(n, h, delta.shape[1])
        ret[c, me] = dsend[c, me]

        @pl.loop(1, n)
        def _(s):
            ret_copy(c, lax.rem(me + s, n), me).start()

    acc[...] = jnp.zeros_like(acc)
    w_copy.wait()

    def add_base(block, owner):
        @pl.loop(0, width // DEPTH)
        def _(i):
            at = pl.multiple_of(i * DEPTH, DEPTH)
            row = pl.multiple_of(owner * width + i * DEPTH, DEPTH)
            acc[...] += jnp.dot(
                block[:, pl.ds(at, DEPTH)], w[pl.ds(row, DEPTH), :], preferred_element_type=jnp.float32)

    def base_across():
        token_copy(1, tok_ref, across, across).wait_recv()
        token_copy(2, gath.at[across], across, sibling).start()
        add_base(gath.at[across], across)

    def base_diagonal():
        token_copy(2, gath.at[across], diagonal, sibling).wait_recv()
        add_base(gath.at[diagonal], diagonal)

    add_base(tok_ref, t)
    token_copy(0, tok_ref, sibling, sibling).wait_recv()
    add_base(gath.at[sibling], sibling)
    down_copy.wait()
    last = pieces - 1
    for c in range(pieces):
        partial(c)
        if c == last // 2:
            base_across()
        if c == last - 1 or last == 0:
            base_diagonal()
        update(c)

    for c in range(pieces):
        @pl.loop(1, n)
        def _(s, c=c):
            j = lax.rem(me + s, n)
            ret_copy(c, j, j).wait_recv()

    back = ret[...].reshape(pieces * rows, out_ref.shape[1])
    change = jnp.dot(comb_ref[...], back, preferred_element_type=jnp.float32)
    out_ref[...] = (acc[...] + change).astype(out_ref.dtype)

    @pl.loop(1, n)
    def _(s):
        j = lax.rem(me + s, n)
        which_copy(j, me).wait_send()
        for c in range(pieces):
            rows_copy(c, j, me).wait_send()
            ret_copy(c, j, me).wait_send()

    for c in range(pieces):
        for k in range(1, 4):
            part_copy(c, k, t, lax.rem(t + k, 4)).wait_send()

    token_copy(0, tok_ref, t, sibling).wait_send()
    token_copy(1, tok_ref, t, across).wait_send()
    token_copy(2, gath.at[across], across, sibling).wait_send()


def shards(
    tokens,
    request_adapter,
    adapter_page_lookup,
    base_key_value_weight,
    down_factor_pages,
    up_factor_pages,
):
    n = lax.axis_size("ad")
    token_rows, width = tokens.shape
    pages, _, rank = down_factor_pages.shape
    columns = base_key_value_weight.shape[1]
    wide = pages * rank
    cap = max(16, min(4 * token_rows // n, token_rows // 2))
    slots = n * cap
    pieces = max(1, min(PIECES, cap // 16))
    h = cap // pieces

    catalog = jnp.arange(adapter_page_lookup.shape[0], dtype=jnp.int32)
    matches = request_adapter[:, None] == catalog[None, :]
    page = jnp.sum(jnp.where(matches, adapter_page_lookup[None, :], 0), axis=1)
    target = page // pages
    within = page % pages
    order = jnp.arange(token_rows, dtype=jnp.int32)
    earlier = (target[:, None] == target[None, :]) & (order[None, :] < order[:, None])
    position = jnp.sum(earlier.astype(jnp.int32), axis=1)
    place = (position // h) * (n * h) + target * h + position % h
    slot = jnp.arange(slots, dtype=jnp.int32)
    dispatch = slot[:, None] == place[None, :]
    combine = (place[:, None] == slot[None, :]).astype(jnp.bfloat16)
    which = jnp.sum(jnp.where(dispatch, within[None, :], 0), axis=1).astype(jnp.bfloat16)
    which = which.reshape(pieces, n, h).transpose(1, 0, 2).reshape(n, 1, cap)
    which = jnp.broadcast_to(which, (n, 16, cap))
    dispatch = dispatch.astype(jnp.bfloat16).reshape(pieces, n * h, token_rows)
    down = jnp.swapaxes(down_factor_pages, 1, 2).reshape(wide, width)

    vmem = pl.BlockSpec(memory_space=pltpu.VMEM)
    hbm = pl.BlockSpec(memory_space=pl.ANY)
    bf16, f32 = jnp.bfloat16, jnp.float32
    dma = pltpu.SemaphoreType.DMA
    return pl.pallas_call(
        functools.partial(kernel, n, pieces, rank),
        out_shape=jax.ShapeDtypeStruct((token_rows, columns), bf16),
        in_specs=[vmem] * 5 + [hbm] * 2,
        out_specs=vmem,
        scratch_shapes=[
            pltpu.VMEM((pieces, n, h, width), bf16),
            pltpu.VMEM((pieces, n, h, width), bf16),
            pltpu.VMEM((n, 16, cap), bf16),
            pltpu.VMEM((4, token_rows, width), bf16),
            pltpu.VMEM(base_key_value_weight.shape, bf16),
            pltpu.VMEM((wide, width), bf16),
            pltpu.VMEM((token_rows, columns), f32),
            pltpu.VMEM((4, pieces, n * h, LANES), f32),
            pltpu.VMEM((pieces, n, h, columns), bf16),
            pltpu.VMEM((pieces, n, h, columns), bf16),
            dma((2,)), dma((pieces, n)), dma((pieces, n)), dma((n,)), dma((n,)),
            dma((3,)), dma((3,)), dma((4, pieces)), dma((4, pieces)),
            dma((pieces, n)), dma((pieces, n)),
        ],
        compiler_params=pltpu.CompilerParams(
            collective_id=0, has_side_effects=True, vmem_limit_bytes=52 * 1024 * 1024
        ),
    )(dispatch, which, tokens, combine, up_factor_pages.reshape(wide, columns),
      base_key_value_weight, down)


def solution(mesh):
    return jax.shard_map(
        shards,
        mesh=mesh,
        in_specs=(
            P(("rep", "ad"), "tp"),
            P(("rep", "ad")),
            P("rep"),
            P(None, "tp"),
            P(("rep", "ad"), "tp", None),
            P(("rep", "ad"), None, "tp"),
        ),
        out_specs=P(("rep", "ad"), "tp"),
        check_vma=False,
    )
```

time: 79.9 us -> 72.3 us (0.905)
  the two profiles are of different devices: /device:TPU:17 before, /device:TPU:0 now
where the time goes in v2:
time: 72.3 us; the launch traced here: 72.1 us
  Pallas kernels  68.7 us (95%)
  local copies, waits for them, and re-layouts  1.93 us (3%)
  other arithmetic  1.4 us (2%)
    pallas_call x1, Pallas kernels, shards(): pl.pallas_call(functools.partial(kernel, n, pieces, rank), out_shape=jax....  68.7 us
    unnamed x3, local copies, waits for them, and re-layouts  1.74 us

profile of v2, /device:TPU:0, one launch (start us, length us, event | category | flops | bytes accessed | tf_op | source)
XLA Modules:
  0.0 72.1 jit_solution(9632513349559014944)
XLA Ops:
  0.0 0.8 %select_reduce_fusion.1 = s32[256]{0:T(256)S(1)} fusion(s32[32]{0:T(128)} %param.8, s32[256]{0:T(256)} %param.7), kind=kLoop, calls=%fused_computation.8 | loop fusion | flops 24320 | bytes 2176 | tf_op jit(solution)/shard_map/reduce_sum | solution.py:218
  0.8 0.2 convert_reduce_fusion
  1.0 0.2 select_reduce_fusion
  1.2 0.1 convert_element_type.20
  1.3 0.1 broadcast_in_dim.47
  1.4 0.1 compare_convert_fusion.disp_ref
  1.5 0.1 fusion.comb_ref
  1.6 0.0 copy-start
  1.6 1.0 %copy-done = bf16[8,64,512]{2,1,0:T(8,128)(2,1)S(1)} copy-done((bf16[8,64,512]{2,1,0:T(8,128)(2,1)S(1)}, bf16[8,64,512]{2,1,0:T(8,128)(2,1)}, u32[]{:S(2)}) %copy-start) | copy-done | bytes 524312
  2.7 68.7 %shard_map.64 = bf16[256,512]{1,0:T(8,128)(2,1)S(1)} custom-call(bf16[4,128,256]{2,1,0:T(8,128)(2,1)S(1)} %compare_convert_fusion.disp_ref, bf16[4,16,128]{2,1,0:T(8,128)(2,1)S(1)} %broadcast_in_dim.48.which_ref, bf16[256,2048]{1,0:T(8,128)(2,1)} %tok_ref.1, bf16[256,512]{1,0:T(8,128)(2,1)S(1)} %fusion.comb_ref, bf16[512,512]{1,0:T(8,128)(2,1)S(1)} %bitcast.5, ...), custom_call_target="tpu_custom_call" | custom-call | tf_op jit(solution)/shard_map/pallas_call | solution.py:238
  71.4 0.7 copy.10
  (6 shorter events, 0.1 us)
Async XLA Ops:
  1.6 1.0 %copy-start = (bf16[8,64,512]{2,1,0:T(8,128)(2,1)S(1)}, bf16[8,64,512]{2,1,0:T(8,128)(2,1)}, u32[]{:S(2)}) copy-start(bf16[8,64,512]{2,1,0:T(8,128)(2,1)} %param.11) | copy-start | bytes 1572868

commit v3 on v2

--- a/solution.py
+++ b/solution.py
@@ -75,10 +75,14 @@
             src_ref=dsend.at[c, j], dst_ref=ret.at[c, slot], send_sem=ret_send.at[c, j],
             recv_sem=ret_recv.at[c, slot], device_id={"ad": j}, device_id_type=MESH)
 
+    def target(i):
+        s = 1 + lax.rem(i + n // 2 + n - 3, n - 1)
+        return lax.rem(me + s + lax.rem(me, 2) * (n - 2 * s), n)
+
     def dispatch(c):
         @pl.loop(1, n)
         def _(s):
-            j = lax.rem(me + s, n)
+            j = target(s)
             if c == 0:
                 which_copy(j, me).start()
             rows_copy(c, j, me).start()
@@ -133,7 +137,7 @@
 
         @pl.loop(1, n)
         def _(s):
-            ret_copy(c, lax.rem(me + s, n), me).start()
+            ret_copy(c, target(s), me).start()
 
     acc[...] = jnp.zeros_like(acc)
     w_copy.wait()

time: 72.3 us -> 71.3 us (0.986)
  Pallas kernels: 68.7 us -> 67.7 us
    pallas_call x1, Pallas kernels: 68.7 us -> 67.7 us  [shards(): pl.pallas_call(functools.partial(kernel, n, pieces, rank), out_shape=jax....]
where the time goes in v3:
time: 71.3 us; the launch traced here: 71.1 us
  Pallas kernels  67.7 us (95%)
  local copies, waits for them, and re-layouts  1.93 us (3%)
  other arithmetic  1.4 us (2%)
    pallas_call x1, Pallas kernels, shards(): pl.pallas_call(functools.partial(kernel, n, pieces, rank), out_shape=jax....  67.7 us
    unnamed x3, local copies, waits for them, and re-layouts  1.74 us

profile of v3, /device:TPU:0, one launch (start us, length us, event | category | flops | bytes accessed | tf_op | source)
XLA Modules:
  0.0 71.1 jit_solution(10289511050135372217)
XLA Ops:
  0.0 0.8 %select_reduce_fusion.1 = s32[256]{0:T(256)S(1)} fusion(s32[32]{0:T(128)} %param.8, s32[256]{0:T(256)} %param.7), kind=kLoop, calls=%fused_computation.8 | loop fusion | flops 24320 | bytes 2176 | tf_op jit(solution)/shard_map/reduce_sum | solution.py:222
  0.8 0.2 convert_reduce_fusion
  1.0 0.2 select_reduce_fusion
  1.2 0.1 convert_element_type.20
  1.3 0.1 broadcast_in_dim.47
  1.4 0.1 compare_convert_fusion.disp_ref
  1.5 0.1 fusion.comb_ref
  1.6 0.0 copy-start
  1.6 1.0 %copy-done = bf16[8,64,512]{2,1,0:T(8,128)(2,1)S(1)} copy-done((bf16[8,64,512]{2,1,0:T(8,128)(2,1)S(1)}, bf16[8,64,512]{2,1,0:T(8,128)(2,1)}, u32[]{:S(2)}) %copy-start) | copy-done | bytes 524312
  2.7 67.7 %shard_map.64 = bf16[256,512]{1,0:T(8,128)(2,1)S(1)} custom-call(bf16[4,128,256]{2,1,0:T(8,128)(2,1)S(1)} %compare_convert_fusion.disp_ref, bf16[4,16,128]{2,1,0:T(8,128)(2,1)S(1)} %broadcast_in_dim.48.which_ref, bf16[256,2048]{1,0:T(8,128)(2,1)} %tok_ref.1, bf16[256,512]{1,0:T(8,128)(2,1)S(1)} %fusion.comb_ref, bf16[512,512]{1,0:T(8,128)(2,1)S(1)} %bitcast.5, ...), custom_call_target="tpu_custom_call" | custom-call | tf_op jit(solution)/shard_map/pallas_call | solution.py:242
  70.4 0.7 copy.10
  (6 shorter events, 0.1 us)
Async XLA Ops:
  1.6 1.0 %copy-start = (bf16[8,64,512]{2,1,0:T(8,128)(2,1)S(1)}, bf16[8,64,512]{2,1,0:T(8,128)(2,1)}, u32[]{:S(2)}) copy-start(bf16[8,64,512]{2,1,0:T(8,128)(2,1)} %param.11) | copy-start | bytes 1572868
